TPU v7x, 32 devices: a whole 2x2x4 slice. The times are simulated.
32 devices in a mesh: dp: 8 (over z, x), tensor: 4 (over y, core).
Axes of the slice: x: 2, y: 2, z: 4, core: 2. Of those that a mesh axis runs over, the one named last changes fastest.
Arguments:
- text_rows: bfloat16 [256, 40, 768], P(('dp', 'tensor')), may hold values from -6 to 6
- patch_features: bfloat16 [256, 145, 1024], P(('dp', 'tensor')), may hold values from -6 to 6
- lengths: int32 [256], P(('dp', 'tensor')), may hold values from 8 to 40, as said below
- text_cotangent: bfloat16 [256, 40, 768], P(('dp', 'tensor')), may hold values from -6 to 6
- join_cotangent: bfloat16 [256, 40, 768], P(('dp', 'tensor')), may hold values from -6 to 6
- text_project_in: bfloat16 [3, 768, 768], P(None, None, 'tensor'), may hold values from -0.21875 to 0.21875
- text_project_bias: bfloat16 [2, 768], P(None, 'tensor'), may hold values from -3 to 3
- text_project_out: bfloat16 [768, 768], P('tensor'), may hold values from -0.75 to 0.75
- text_expand: bfloat16 [768, 3072], P(None, 'tensor'), may hold values from -0.21875 to 0.21875
- text_expand_bias: bfloat16 [3072], P('tensor'), may hold values from -3 to 3
- text_contract: bfloat16 [3072, 768], P('tensor'), may hold values from -0.109375 to 0.109375
- text_out_bias: bfloat16 [2, 768], replicated, may hold values from -3 to 3
- text_norm_gain: bfloat16 [2, 768], replicated, may hold values from 0.099609375 to 1.8984375
- text_norm_shift: bfloat16 [2, 768], replicated, may hold values from -3 to 3
- join_project_in: bfloat16 [4, 768, 768], P(None, None, 'tensor'), may hold values from -0.21875 to 0.21875
- join_project_bias: bfloat16 [4, 768], P(None, 'tensor'), may hold values from -3 to 3
- join_project_out: bfloat16 [768, 768], P('tensor'), may hold values from -0.75 to 0.75
- cross_project_out: bfloat16 [768, 768], P('tensor'), may hold values from -1.5 to 1.5
- cross_key_value: bfloat16 [2, 1024, 768], P(None, None, 'tensor'), may hold values from -0.1875 to 0.1875
- join_expand: bfloat16 [768, 3072], P(None, 'tensor'), may hold values from -0.21875 to 0.21875
- join_expand_bias: bfloat16 [3072], P('tensor'), may hold values from -3 to 3
- join_contract: bfloat16 [3072, 768], P('tensor'), may hold values from -0.109375 to 0.109375
- join_out_bias: bfloat16 [3, 768], replicated, may hold values from -3 to 3
- join_norm_gain: bfloat16 [3, 768], replicated, may hold values from 0.099609375 to 1.8984375
- join_norm_shift: bfloat16 [3, 768], replicated, may hold values from -3 to 3
Outputs:
- text_out: bfloat16 [256, 40, 768], P(('dp', 'tensor'))
- join_out: bfloat16 [256, 40, 768], P(('dp', 'tensor'))
- grad_text: bfloat16 [256, 40, 768], P(('dp', 'tensor'))
- grad_patches: bfloat16 [256, 145, 1024], P(('dp', 'tensor'))
- grad_text_project_in: float32 [3, 768, 768], P(None, None, 'tensor')
- grad_text_project_bias: float32 [2, 768], P(None, 'tensor')
- grad_text_project_out: float32 [768, 768], P('tensor')
- grad_text_expand: float32 [768, 3072], P(None, 'tensor')
- grad_text_expand_bias: float32 [3072], P('tensor')
- grad_text_contract: float32 [3072, 768], P('tensor')
- grad_text_out_bias: float32 [2, 768], replicated
- grad_text_norm_gain: float32 [2, 768], replicated
- grad_text_norm_shift: float32 [2, 768], replicated
- grad_join_project_in: float32 [4, 768, 768], P(None, None, 'tensor')
- grad_join_project_bias: float32 [4, 768], P(None, 'tensor')
- grad_join_project_out: float32 [768, 768], P('tensor')
- grad_cross_project_out: float32 [768, 768], P('tensor')
- grad_cross_key_value: float32 [2, 1024, 768], P(None, None, 'tensor')
- grad_join_expand: float32 [768, 3072], P(None, 'tensor')
- grad_join_expand_bias: float32 [3072], P('tensor')
- grad_join_contract: float32 [3072, 768], P('tensor')
- grad_join_out_bias: float32 [3, 768], replicated
- grad_join_norm_gain: float32 [3, 768], replicated
- grad_join_norm_shift: float32 [3, 768], replicated
Inputs may be any that keep to these rules, and one draw needn't show every extreme that they name: An item's first lengths slots hold its text, the others padding; in every draw some item has all 40 slots real and some item only 8.
All inputs are finite; a program needn't handle non-finite values.
Results may differ from a plain program's by a relative error of at most 0.029.
Values may be sent and summed in bfloat16 or wider, within the bound.
A program may use at most 256 MiB of HBM per device.

v0:
```python
import functools

import jax
import jax.numpy as jnp
from jax import lax
from jax.experimental import pallas as pl
from jax.experimental.pallas import tpu as pltpu
from jax.sharding import PartitionSpec as P

HEAD_DIM = 64
BF = jnp.bfloat16
F32 = jnp.float32
ANY = pl.ANY


def dot_nn(a, b):
    return lax.dot_general(a, b, (((1,), (0,)), ((), ())), preferred_element_type=F32)


def dot_nt(a, b):
    return lax.dot_general(a, b, (((1,), (1,)), ((), ())), preferred_element_type=F32)


def dot_tn(a, b):
    return lax.dot_general(a, b, (((0,), (0,)), ((), ())), preferred_element_type=F32)


def norm_forward(e, gain, shift):
    center = e - jnp.mean(e, axis=-1, keepdims=True)
    variance = jnp.mean(center * center, axis=-1, keepdims=True)
    return center * lax.rsqrt(variance + 1e-12) * gain + shift


def norm_backward(e, gain, dy):
    center = e - jnp.mean(e, axis=-1, keepdims=True)
    variance = jnp.mean(center * center, axis=-1, keepdims=True)
    rstd = lax.rsqrt(variance + 1e-12)
    normed = center * rstd
    scaled = dy * gain
    de = rstd * (
        scaled
        - jnp.mean(scaled, axis=-1, keepdims=True)
        - normed * jnp.mean(scaled * normed, axis=-1, keepdims=True)
    )
    sums = jnp.concatenate(
        [
            jnp.sum(de, axis=0, keepdims=True),
            jnp.sum(dy * normed, axis=0, keepdims=True),
            jnp.sum(dy, axis=0, keepdims=True),
        ],
        axis=0,
    )
    return de, sums


def head_masks(width):
    lane = lax.broadcasted_iota(jnp.int32, (1, width), 1)
    return [
        ((lane >= h * HEAD_DIM) & (lane < (h + 1) * HEAD_DIM)).astype(F32)
        for h in range(width // HEAD_DIM)
    ]


def stack_heads(rows, masks):
    return jnp.concatenate([rows * mask for mask in masks], axis=0).astype(BF)


def merge_heads(stacked, masks):
    count = stacked.shape[0] // len(masks)
    total = stacked[:count] * masks[0]
    for h in range(1, len(masks)):
        total = total + stacked[h * count : (h + 1) * count] * masks[h]
    return total


def item_forward(q, k, v, masks, length):
    scores = dot_nt(stack_heads(q, masks), k) * HEAD_DIM ** (-0.5)
    column = lax.broadcasted_iota(jnp.int32, scores.shape, 1)
    scores = jnp.where(column < length, scores, -1e30)
    weights = jnp.exp(scores - jnp.max(scores, axis=-1, keepdims=True))
    probs = (weights / jnp.sum(weights, axis=-1, keepdims=True)).astype(BF)
    return probs, merge_heads(dot_nn(probs, v), masks)


def item_backward(q, k, v, da, probs, masks):
    qs = stack_heads(q, masks)
    das = stack_heads(da, masks)
    dv = dot_tn(probs, das)
    dp = dot_nt(das, v)
    p = probs.astype(F32)
    ds = (p * (dp - jnp.sum(p * dp, axis=-1, keepdims=True))).astype(BF)
    scaling = HEAD_DIM ** (-0.5)
    dq = merge_heads(dot_nn(ds, k), masks) * scaling
    dk = dot_tn(ds, qs) * scaling
    return dq, dk, dv


def pair(index, width):
    return index + width - 2 * width * ((index // width) % 2)


def rest(m, n):
    return m % n if isinstance(m, int) else lax.rem(m, n)


def when(condition, act):
    if isinstance(condition, bool):
        if condition:
            act()
    else:
        pl.when(condition)(act)


def halvings(n_dp, chunk):
    return min(n_dp, chunk // 16).bit_length() - 1


class Sums:
    def __init__(self, n_tensor, n_dp, counts, chunk, sends, keeps, outs, small, scratch):
        self.n_dp, self.bits = n_dp, n_dp.bit_length() - 1
        self.counts, self.chunk = counts, chunk
        self.cuts = halvings(n_dp, chunk)
        self.sends, self.keeps, self.outs = sends, keeps, outs
        self.small_send, self.small_keep, self.small_out = small
        scratch = list(scratch)
        bits = self.bits
        self.core_in, self.kept, self.far_out, self.far_in, self.own, self.whole = scratch[:6]
        self.parts, self.halves = scratch[6 : 6 + bits], scratch[6 + bits : 6 + 2 * bits]
        self.gathered, self.tiny_sum, self.tiny_core, self.tiny_far, self.tiny_dp = scratch[
            6 + 2 * bits : 11 + 2 * bits
        ]
        self.send_sem, self.recv_sem, self.kept_sem, self.out_sem = scratch[
            11 + 2 * bits : 15 + 2 * bits
        ]
        self.tiny_send, self.tiny_recv = scratch[15 + 2 * bits :]
        t, d = lax.axis_index("tensor"), lax.axis_index("dp")
        self.dp_bits = [(d // (1 << b)) % 2 for b in range(bits)]
        self.peers = [{"tensor": pair(t, 1)}, {"tensor": lax.rem(t + 2, n_tensor)}]
        self.peers += [{"dp": pair(d, 1 << b)} for b in range(bits)]
        self.total = sum(counts)
        self.stages = 2 + bits + self.cuts
        self.slots, self.depth = self.core_in.shape[0], self.gathered.shape[0]

    def greet(self):
        barrier = pltpu.get_barrier_semaphore()
        for peer in self.peers:
            pl.semaphore_signal(
                barrier, inc=1, device_id=peer, device_id_type=pl.DeviceIdType.MESH
            )
        pl.semaphore_wait(barrier, len(self.peers))

    def remote(self, source, target, stage, slot, peer):
        return pltpu.make_async_remote_copy(
            src_ref=source,
            dst_ref=target,
            send_sem=self.send_sem.at[stage, slot],
            recv_sem=self.recv_sem.at[stage, slot],
            device_id=self.peers[peer],
            device_id_type=pl.DeviceIdType.MESH,
        )

    def region(self, b):
        b = min(b, self.cuts - 1)
        size = self.chunk >> (b + 1)
        start = 0
        for i in range(b + 1):
            start = start + self.dp_bits[i] * (self.chunk >> (i + 1))
        return pl.ds(pl.multiple_of(start, size), size)

    def half(self, b, mine):
        if b >= self.cuts:
            return pl.ds(0, self.chunk >> self.cuts)
        size = self.chunk >> (b + 1)
        which = self.dp_bits[b] if mine else 1 - self.dp_bits[b]
        return pl.ds(pl.multiple_of(which * size, size), size)

    def halved(self, b):
        return self.whole if b == 0 else self.parts[b - 1]

    def copy_of(self, stage, m):
        slot, two = rest(m, self.slots), rest(m, 2)
        if stage == 0:
            source = self.sends[0].at[:, pl.ds(0, self.chunk)]
            return self.remote(source, self.core_in.at[slot], 0, slot, 0)
        if stage == 1:
            ring = rest(m, self.far_in.shape[0])
            return self.remote(self.far_out.at[slot], self.far_in.at[ring], 1, ring, 1)
        if stage < 2 + self.bits:
            b = stage - 2
            source = self.halved(b).at[two, self.half(b, False)]
            return self.remote(source, self.halves[b].at[slot], stage, slot, 2 + b)
        b = 1 + self.bits + self.cuts - stage
        held = self.gathered.at[rest(m, self.depth), self.region(b)]
        return self.remote(held, held, stage, slot, 2 + b)

    def kept_copy(self, a, start, m):
        two = rest(m, 2)
        source = self.keeps[a].at[:, pl.ds(start, self.chunk)]
        return pltpu.make_async_copy(source, self.kept.at[two], self.kept_sem.at[two])

    def out_copy(self, a, start, m):
        ring = rest(m, self.depth)
        target = self.outs[a].at[pl.ds(start, self.chunk)]
        return pltpu.make_async_copy(self.gathered.at[ring], target, self.out_sem.at[ring])

    def each_array(self, m, act):
        base = 0
        for a, count in enumerate(self.counts):
            if isinstance(m, int):
                start = (m - base) * self.chunk
                inside = base <= m < base + count
            else:
                start = pl.multiple_of((m - base) * self.chunk, self.chunk)
                inside = (m >= base) & (m < base + count)
            when(inside, functools.partial(act, a, start))
            base += count

    def process(self, step, m):
        if step == 2:
            return
        stage = step if step < 2 else step - 1
        slot, two, ring = rest(m, self.slots), rest(m, 2), rest(m, self.depth)
        stages, bits = self.stages, self.bits
        if stage == 0:

            def begin(a, start):
                source = self.sends[a].at[:, pl.ds(start, self.chunk)]
                self.remote(source, self.core_in.at[slot], 0, slot, 0).start()
                self.kept_copy(a, start, m).start()

            self.each_array(m, begin)
            return
        if stage <= stages:
            self.copy_of(stage - 1, m).wait()
        if stage == 1:
            self.kept_copy(0, 0, m).wait()
            self.far_out[slot] = self.kept[two, 1] + self.core_in[slot, 1]
            self.own[slot] = self.kept[two, 0] + self.core_in[slot, 0]
        elif stage == 2:
            self.whole[two] = self.own[slot] + self.far_in[rest(m, self.far_in.shape[0])]
        elif stage <= 2 + bits:
            b = stage - 3
            summed = self.halved(b)[two, self.half(b, True)] + self.halves[b][slot]
            if b < bits - 1:
                self.parts[b][two] = summed
            else:
                self.gathered[ring, self.region(b)] = summed
        elif stage == stages:
            self.each_array(m, lambda a, start: self.out_copy(a, start, m).start())
        elif stage == stages + 1:
            self.out_copy(0, 0, m).wait()
        if stage < stages:
            self.copy_of(stage, m).start()

    def tiny(self, stage):
        count = self.tiny_far.shape[0]
        if stage == 0:
            source, target = self.small_send, self.tiny_core
        elif stage == 1:
            first = self.small_keep.shape[0] - count
            source, target = self.tiny_sum.at[0, pl.ds(first, count)], self.tiny_far
        else:
            source = self.tiny_sum.at[stage - 1, pl.ds(0, count)]
            target = self.tiny_dp.at[stage - 2]
        return pltpu.make_async_remote_copy(
            src_ref=source,
            dst_ref=target,
            send_sem=self.tiny_send.at[stage],
            recv_sem=self.tiny_recv.at[stage],
            device_id=self.peers[stage],
            device_id_type=pl.DeviceIdType.MESH,
        )

    def tiny_step(self, stage):
        bits = self.bits
        count = self.tiny_far.shape[0]
        units = self.small_keep.shape[0] - count
        if stage > 0:
            self.tiny(stage - 1).wait()
        if stage == 1:
            self.tiny_sum[0] = self.small_keep[...] + self.tiny_core[...]
        elif stage == 2:
            self.tiny_sum[1, 0:units] = self.tiny_sum[0, 0:units] + self.tiny_far[0:units]
            self.tiny_sum[1, units:count] = (
                self.tiny_sum[0, 2 * units :] + self.tiny_far[units:]
            )
        elif stage > 2:
            summed = self.tiny_sum[stage - 2, 0:count] + self.tiny_dp[stage - 3]
            if stage == 2 + bits:
                self.small_out[...] = summed
            else:
                self.tiny_sum[stage - 1, 0:count] = summed
        if stage < 2 + bits:
            self.tiny(stage).start()

    def tick(self, k):
        for step in range(self.stages + 3):
            m = k - step
            inside = (m >= 0) & (m < self.total)
            when(inside, functools.partial(self.process, step, m))

    def finish(self, first):
        def step(k, carry):
            self.tick(k)
            for stage in range(3 + self.bits):
                when(k == first + stage, functools.partial(self.tiny_step, stage))
            return carry

        lax.fori_loop(first, self.total + self.stages + 3, step, 0)

    @staticmethod
    def scratch(n_dp, chunk, model, small, units):
        bits, cuts = n_dp.bit_length() - 1, halvings(n_dp, chunk)
        slots, far, depth, stages = 4, 6, 8, 2 + bits + cuts
        sizes = [chunk >> min(b + 1, cuts) for b in range(bits)]
        return (
            [
                pltpu.VMEM((slots, 2, chunk, model), BF),
                pltpu.VMEM((2, 2, chunk, model), BF),
                pltpu.VMEM((slots, chunk, model), BF),
                pltpu.VMEM((far, chunk, model), BF),
                pltpu.VMEM((slots, chunk, model), BF),
                pltpu.VMEM((2, chunk, model), BF),
            ]
            + [pltpu.VMEM((2, size, model), BF) for size in sizes]
            + [pltpu.VMEM((slots, size, model), BF) for size in sizes]
            + [
                pltpu.VMEM((depth, chunk, model), BF),
                pltpu.VMEM((1 + bits, small, model), F32),
                pltpu.VMEM((small, model), F32),
                pltpu.VMEM((small - units, model), F32),
                pltpu.VMEM((bits, small - units, model), F32),
                pltpu.SemaphoreType.DMA((stages, far)),
                pltpu.SemaphoreType.DMA((stages, far)),
                pltpu.SemaphoreType.DMA((2,)),
                pltpu.SemaphoreType.DMA((depth,)),
                pltpu.SemaphoreType.DMA((2 + bits,)),
                pltpu.SemaphoreType.DMA((2 + bits,)),
            ]
        )


class Flow:
    def __init__(self, net, a, lo, hi, spread):
        rows = hi - lo
        own, got = net.own[a], net.got[a]
        here = pl.ds(lo, rows)
        self.copies = []
        self.started = self.waited = 0
        if spread and rows % (16 * net.n_dp) == 0:

            def region(count):
                size, start = rows, lo
                for i in range(count):
                    size //= 2
                    start = start + net.dp_bits[i] * size
                return pl.ds(pl.multiple_of(start, 16), size)

            part = region(net.bits)
            self.add(net, own.at[part], got.at[1, part], net.far_peer)
            for b in reversed(range(net.bits)):
                part = region(b + 1)
                self.add(net, got.at[1, part], got.at[1, part], net.dp_peers[b])
        else:
            self.add(net, own.at[here], got.at[1, here], net.far_peer)
        self.add(net, got.at[1, here], got.at[2, here], net.core_peer)

    def add(self, net, source, target, peer):
        self.copies.append(net.remote(source, target, peer))

    def advance(self):
        if self.started < len(self.copies):
            if self.started > 0:
                self.await_copy(self.started - 1)
            self.copies[self.started].start()
            self.started += 1

    def await_copy(self, n):
        while self.started <= n:
            self.advance()
        while self.waited <= n:
            self.copies[self.waited].wait_recv()
            self.waited += 1

    def need(self, r):
        self.await_copy(len(self.copies) - (2 if r == 2 else 1))

    def close(self):
        self.need(3)
        for copy in self.copies:
            copy.wait_send()


class Direct:
    def __init__(self, copy):
        self.copy, self.state = copy, 0

    def advance(self):
        if self.state == 0:
            self.copy.start()
            self.state = 1

    def need(self):
        self.advance()
        if self.state == 1:
            self.copy.wait_recv()
            self.state = 2

    def close(self):
        self.need()
        self.copy.wait_send()


class Net:
    def __init__(self, n_tensor, n_dp, own, got, send_sem, recv_sem):
        self.n_dp, self.bits = n_dp, n_dp.bit_length() - 1
        self.own, self.got = own, got
        self.send_sem, self.recv_sem = send_sem, recv_sem
        self.count = 0
        t, d = lax.axis_index("tensor"), lax.axis_index("dp")
        self.core_peer = {"tensor": pair(t, 1)}
        self.far_peer = {"tensor": lax.rem(t + 2, n_tensor)}
        self.dp_peers = [{"dp": pair(d, 1 << b)} for b in range(self.bits)]
        self.dp_bits = [(d // (1 << b)) % 2 for b in range(self.bits)]
        peers = [self.core_peer, self.far_peer] + self.dp_peers
        barrier = pltpu.get_barrier_semaphore()
        for peer in peers:
            pl.semaphore_signal(
                barrier, inc=1, device_id=peer, device_id_type=pl.DeviceIdType.MESH
            )
        pl.semaphore_wait(barrier, len(peers))

    def remote(self, source, target, peer):
        n = self.count
        self.count += 1
        return pltpu.make_async_remote_copy(
            src_ref=source,
            dst_ref=target,
            send_sem=self.send_sem.at[n],
            recv_sem=self.recv_sem.at[n],
            device_id=peer,
            device_id_type=pl.DeviceIdType.MESH,
        )


TEXT_IN, TEXT_OUT, EXPAND_ONE, CONTRACT_ONE, JOIN_IN = range(5)
JOIN_OUT, KEY_VALUE, CROSS_OUT, EXPAND_TWO, CONTRACT_TWO = range(5, 10)
ARRAYS = 10


def spread_patches(source, wide, target, items, padded):
    patches = source.shape[0]
    least = patches // 8 * 8
    groups, _, lanes = wide.shape
    for i in range(items):
        rows = pl.ds(i * padded + least, padded - least)
        wide[:, rows] = jnp.zeros((groups, padded - least, lanes), F32)

    def step(n, carry):
        for c in range(groups):
            wide[c, pl.ds(n, items, stride=padded)] = source[
                n, :, c * lanes : (c + 1) * lanes
            ].astype(F32)
        return carry

    lax.fori_loop(0, patches, step, 0)
    for c in range(groups):
        target[:, c * lanes : (c + 1) * lanes] = wide[c].astype(BF)


def norm_rows(vecs, text, join):
    for c in range(3):
        for n in range(2):
            vecs[n, c : c + 1] = text[c][...].astype(F32)[n : n + 1]
        for n in range(3):
            vecs[2 + n, c : c + 1] = join[c][...].astype(F32)[n : n + 1]


def forward_kernel(sizes, *refs):
    n_tensor, n_dp, items, slots, patches, padded, width = sizes
    refs = list(refs)

    def take(n):
        got, refs[:n] = refs[:n], []
        return got

    own = take(ARRAYS)
    bias_in, vecs_in = take(4), take(6)
    lengths, x, pf_in = take(3)
    got = take(ARRAYS)
    text_out, join_out, e_out, pf_out = take(4)
    self_out = [take(5), take(5)]
    cross_out = take(5)
    feed_out = [take(2), take(2)]
    ws, wf, wc, wk, acc, u, ub, e_s = take(8)
    pf_raw, pf_wide, pf, vecs = take(4)
    q_st, k_st, v_st, a_st, p_st = self_st = take(5)
    cross_st = take(5)
    qc_st, kc_st, vc_st, ac_st, pc_st = cross_st
    h_st, slope_st = feed_st = take(2)
    q_s, k_s, v_s, a_s, bias = take(5)
    send_sem, recv_sem, fetch_sem, store_sem, pf_sem = take(5)
    model = x.shape[1]
    hidden = own[EXPAND_ONE].shape[1]

    pf_copy = pltpu.make_async_copy(pf_in, pf_raw, pf_sem)
    pf_copy.start()
    net = Net(n_tensor, n_dp, own, got, send_sem, recv_sem)
    middle = 2 * width
    flows = {
        "s1p": Flow(net, TEXT_IN, 0, middle, True),
        "s1v": Flow(net, TEXT_IN, middle, 3 * width, False),
        "s1o": Flow(net, TEXT_OUT, 0, width, False),
        "e1": Flow(net, EXPAND_ONE, 0, model, True),
        "k1": Flow(net, CONTRACT_ONE, 0, hidden, True),
        "s2p": Flow(net, JOIN_IN, 0, middle, True),
        "s2v": Flow(net, JOIN_IN, middle, 3 * width, False),
        "s2o": Flow(net, JOIN_OUT, 0, width, False),
        "ckv": Flow(net, KEY_VALUE, 0, middle, False),
        "cq": Flow(net, JOIN_IN, 3 * width, 4 * width, False),
        "co": Flow(net, CROSS_OUT, 0, width, False),
        "e2": Flow(net, EXPAND_TWO, 0, model, True),
        "k2": Flow(net, CONTRACT_TWO, 0, hidden, True),
    }
    near = [Direct(net.remote(own[a], got[a].at[0], net.core_peer)) for a in range(ARRAYS)]
    bias_near = Direct(net.remote(bias.at[0], bias.at[1], net.core_peer))
    bias_far = Direct(net.remote(bias.at[0], bias.at[2], net.far_peer))
    bias_last = Direct(net.remote(bias.at[2], bias.at[3], net.core_peer))

    def move(names):
        for name in names.split():
            flows[name].advance()

    fetches = {}

    fetch_count = [0]

    def fetch(key, r, wanted):
        if key in fetches:
            return
        fetches[key] = []
        for a, lo, hi, target, names in wanted:
            if r == 1:
                near[a].need()
            elif r > 1:
                for name in names:
                    flows[name].need(r)
            source = own[a] if r == 0 else got[a].at[r - 1]
            copy = pltpu.make_async_copy(
                source.at[pl.ds(lo, hi - lo)], target, fetch_sem.at[fetch_count[0]]
            )
            fetch_count[0] += 1
            copy.start()
            fetches[key].append(copy)

    def arrive(key):
        for copy in fetches[key]:
            copy.wait()

    stores = []

    def store(source, target):
        copy = pltpu.make_async_copy(source, target, store_sem.at[len(stores)])
        copy.start()
        stores.append(copy)
        return len(stores) - 1

    masks = head_masks(width)
    pending = {"self": [], "feed": []}

    def settle(kind):
        for n in pending[kind]:
            stores[n].wait()
            stores[n] = None
        pending[kind] = []

    def close_layer(n, target=None):
        e = acc[...]
        e_s[n] = e
        store(e_s.at[n], e_out.at[n])
        y = norm_forward(e, vecs[n, 1:2], vecs[n, 2:3])
        if target is not None:
            yb = y.astype(BF)
            target[...] = yb
            ub[...] = yb
            u[...] = yb.astype(F32)
        else:
            u[...] = y
            ub[...] = y.astype(BF)

    def open_layer(n):
        acc[...] = u[...] + vecs[n, 0:1]

    def fetch_self(layer, r):
        first = pl.ds(0, 3 * width)
        last = pl.ds(3 * width, width)
        if layer == 0:
            wanted = [
                (TEXT_IN, 0, 3 * width, ws.at[r, first], ("s1p", "s1v")),
                (TEXT_OUT, 0, width, ws.at[r, last], ("s1o",)),
            ]
        else:
            wanted = [
                (JOIN_IN, 0, 3 * width, ws.at[r, first], ("s2p", "s2v")),
                (JOIN_OUT, 0, width, ws.at[r, last], ("s2o",)),
            ]
        fetch(("self", layer, r), r, wanted)

    def self_unit(layer, r):
        fetch_self(layer, r)
        arrive(("self", layer, r))
        xb = ub[...]
        q = (
            dot_nt(xb, ws[r, 0:width]) + bias[r, 2 * layer : 2 * layer + 1, 0:width]
        ).astype(BF)
        k = dot_nt(xb, ws[r, width : 2 * width]).astype(BF)
        v = (
            dot_nt(xb, ws[r, 2 * width : 3 * width])
            + bias[r, 2 * layer + 1 : 2 * layer + 2, 0:width]
        ).astype(BF)
        q_st[r], k_st[r], v_st[r] = q, k, v
        q_s[...], k_s[...], v_s[...] = q.astype(F32), k.astype(F32), v.astype(F32)
        for i in range(items):
            rows = pl.ds(i * slots, slots)
            probs, a = item_forward(
                q_s[rows], k_s[rows].astype(BF), v_s[rows].astype(BF), masks, lengths[i]
            )
            p_st[r, i] = probs
            a_s[rows] = a
        ab = a_s[...].astype(BF)
        a_st[r] = ab
        acc[...] += dot_nn(ab, ws[r, 3 * width : 4 * width])

    def self_close(layer):
        for source, target in zip(self_st, self_out[layer]):
            pending["self"].append(store(source, target))

    def fetch_feed(layer, r, late=False):
        a = (EXPAND_ONE, EXPAND_TWO)[layer]
        fetch(("expand", layer, r), r, [(a, 0, model, wf.at[r, 0], (("e1", "e2")[layer],))])
        if not late:
            fetch_contract(layer, r)

    def fetch_contract(layer, r):
        b = (CONTRACT_ONE, CONTRACT_TWO)[layer]
        name = ("k1", "k2")[layer]
        fetch(("contract", layer, r), r, [(b, 0, hidden, wf.at[r, 1], (name,))])

    def feed_unit(layer, r):
        fetch_feed(layer, r, True)
        arrive(("expand", layer, r))
        z = dot_nn(ub[...], wf[r, 0]) + bias[r, 6 + layer : 7 + layer, 0:hidden]
        cdf = 0.5 * (1.0 + lax.erf(z * 0.7071067811865476))
        slope = cdf + z * (jnp.exp(-0.5 * z * z) * 0.3989422804014327)
        h = (z * cdf).astype(BF)
        h_st[r] = h
        slope_st[r] = slope.astype(BF)
        fetch_contract(layer, r)
        arrive(("contract", layer, r))
        acc[...] += dot_nn(h, wf[r, 1])

    def feed_close(layer):
        for source, target in zip(feed_st, feed_out[layer]):
            pending["feed"].append(store(source, target))

    def fetch_keys(r):
        fetch(("keys", r), r, [(KEY_VALUE, 0, middle, wk.at[r], ("ckv",))])

    def keys_unit(r):
        fetch_keys(r)
        arrive(("keys", r))
        chunk = 2 * padded
        for m in range(items // 2):
            rows = slice(m * chunk, (m + 1) * chunk)
            kc_st[r, rows] = dot_nt(pf[rows], wk[r, 0:width]).astype(BF)
            vc_st[r, rows] = (
                dot_nt(pf[rows], wk[r, width:middle]) + bias[r, 5:6, 0:width]
            ).astype(BF)

    def fetch_cross(r):
        wanted = [
            (JOIN_IN, 3 * width, 4 * width, wc.at[r, pl.ds(0, width)], ("cq",)),
            (CROSS_OUT, 0, width, wc.at[r, pl.ds(width, width)], ("co",)),
        ]
        fetch(("cross", r), r, wanted)

    def cross_unit(r):
        fetch_cross(r)
        arrive(("cross", r))
        q = (dot_nt(ub[...], wc[r, 0:width]) + bias[r, 4:5, 0:width]).astype(BF)
        qc_st[r] = q
        q_s[...] = q.astype(F32)
        for i in range(items):
            rows = pl.ds(i * slots, slots)
            keys = pl.ds(i * padded, padded)
            probs, a = item_forward(q_s[rows], kc_st[r, keys], vc_st[r, keys], masks, patches)
            pc_st[r, i] = probs
            a_s[rows] = a
        ab = a_s[...].astype(BF)
        ac_st[r] = ab
        acc[...] += dot_nn(ab, wc[r, width:middle])

    def near_start(*arrays):
        for a in arrays:
            near[a].advance()

    move("s1p e1 k1")
    near_start(TEXT_IN, TEXT_OUT)
    bias[0] = jnp.zeros(bias.shape[1:], F32)
    bias[0, 0:2, 0:width] = bias_in[0][...].astype(F32)
    bias[0, 2:6, 0:width] = bias_in[1][...].astype(F32)
    bias[0, 6:7] = bias_in[2][...].astype(F32).reshape(1, hidden)
    bias[0, 7:8] = bias_in[3][...].astype(F32).reshape(1, hidden)
    bias_near.advance()
    bias_far.advance()
    near_start(KEY_VALUE)
    fetch_self(0, 0)
    fetch_keys(0)
    norm_rows(vecs, vecs_in[0:3], vecs_in[3:6])
    u[...] = x[...].astype(F32)
    ub[...] = x[...]
    open_layer(0)
    self_unit(0, 0)
    move("s1p s1v s1o")
    bias_near.need()
    fetch_self(0, 1)
    self_unit(0, 1)
    move("e1 s1p k1")
    bias_far.need()
    bias_last.advance()
    near_start(EXPAND_ONE, CONTRACT_ONE)
    pf_copy.wait()
    spread_patches(pf_raw, pf_wide, pf, items, padded)
    store(pf, pf_out)
    keys_unit(0)
    move("s1p e1")
    fetch_keys(1)
    keys_unit(1)
    move("k1 s2p e1 s1p")
    bias_last.need()
    move("s1v s1o ckv")
    near_start(JOIN_IN, JOIN_OUT)
    fetch_self(0, 2)
    fetch_self(0, 3)
    self_unit(0, 2)
    fetch_feed(0, 0)
    self_unit(0, 3)
    self_close(0)
    close_layer(0)
    open_layer(1)
    move("k1 s2p e2 k2")
    fetch_feed(0, 1)
    feed_unit(0, 0)
    feed_unit(0, 1)
    move("e1 s2p e2 k2")
    fetch_feed(0, 2, True)
    fetch_feed(0, 3, True)
    move("s2p e2 ckv s2v s2o")
    fetch_keys(2)
    fetch_keys(3)
    keys_unit(2)
    keys_unit(3)
    for source, target in zip(cross_st[1:3], cross_out[1:3]):
        store(source, target)
    move("k1 e2")
    near_start(CROSS_OUT, EXPAND_TWO, CONTRACT_TWO)
    fetch_contract(0, 2)
    fetch_contract(0, 3)
    feed_unit(0, 2)
    fetch_self(1, 0)
    feed_unit(0, 3)
    feed_close(0)
    close_layer(1, text_out)
    open_layer(2)
    settle("self")
    move("s2p k2 cq co")
    fetch_self(1, 1)
    self_unit(1, 0)
    self_unit(1, 1)
    move("s2v s2o k2")
    fetch_self(1, 2)
    fetch_self(1, 3)
    self_unit(1, 2)
    fetch_cross(0)
    self_unit(1, 3)
    self_close(1)
    close_layer(2)
    open_layer(3)
    move("e2")
    fetch_cross(1)
    cross_unit(0)
    fetch_feed(1, 0)
    cross_unit(1)
    move("cq co")
    fetch_cross(2)
    fetch_cross(3)
    cross_unit(2)
    fetch_feed(1, 1)
    cross_unit(3)
    for n in (0, 3, 4):
        store(cross_st[n], cross_out[n])
    close_layer(3)
    open_layer(4)
    settle("feed")
    move("k2")
    fetch_feed(1, 2, True)
    fetch_feed(1, 3, True)
    feed_unit(1, 0)
    feed_unit(1, 1)
    feed_unit(1, 2)
    feed_unit(1, 3)
    feed_close(1)
    close_layer(4, join_out)

    for copy in stores:
        if copy is not None:
            copy.wait()
    for flow in flows.values():
        flow.close()
    for direct in near + [bias_near, bias_far, bias_last]:
        direct.close()


def forward_all(links, own, biases, vecs, lengths, x, patch_rows, width):
    patches, items, features = patch_rows.shape
    rows, model = x.shape
    slots, padded = rows // items, -(-patches // 16) * 16
    hidden = own[EXPAND_ONE].shape[1]
    heads = width // HEAD_DIM
    anywhere = pl.BlockSpec(memory_space=ANY)
    vmem = pl.BlockSpec(memory_space=pltpu.VMEM)
    sizes = (links.tensor, links.dp, items, slots, patches, padded, width)
    mid = ((4, rows, width), BF)
    key = ((4, items * padded, width), BF)
    probs = ((4, items, heads * slots, slots), BF)
    cross_probs = ((4, items, heads * slots, padded), BF)
    feed = ((4, rows, hidden), BF)
    pf = ((items * padded, features), BF)
    self_kept = [mid] * 4 + [probs]
    cross_kept = [mid, key, key, mid, cross_probs]
    kept = self_kept * 2 + cross_kept + [feed] * 4
    outputs = [((3,) + a.shape, BF) for a in own]
    outputs += [((rows, model), BF)] * 2 + [((5, rows, model), F32), pf] + kept
    remotes = 13 * (2 + links.bits) + ARRAYS + 3
    outs = pl.pallas_call(
        functools.partial(forward_kernel, sizes),
        in_specs=[anywhere] * ARRAYS
        + [vmem] * 10
        + [pl.BlockSpec(memory_space=pltpu.SMEM), vmem, anywhere],
        out_specs=[anywhere] * ARRAYS + [vmem] * 2 + [anywhere] * (2 + len(kept)),
        out_shape=[jax.ShapeDtypeStruct(shape, dtype) for shape, dtype in outputs],
        scratch_shapes=[
            pltpu.VMEM((4, 4 * width, model), BF),
            pltpu.VMEM((4, 2, model, hidden), BF),
            pltpu.VMEM((4, 2 * width, model), BF),
            pltpu.VMEM((4, 2 * width, features), BF),
            pltpu.VMEM((rows, model), F32),
            pltpu.VMEM((rows, model), F32),
            pltpu.VMEM((rows, model), BF),
            pltpu.VMEM((5, rows, model), F32),
            pltpu.VMEM(patch_rows.shape, BF),
            pltpu.VMEM((features // 128, items * padded, 128), F32),
            pltpu.VMEM(*pf),
            pltpu.VMEM((5, 3, model), F32),
        ]
        + [pltpu.VMEM(*item) for item in self_kept + cross_kept + [feed] * 2]
        + [pltpu.VMEM((rows, width), F32)] * 4
        + [
            pltpu.VMEM((4, 8, model), F32),
            pltpu.SemaphoreType.DMA((remotes,)),
            pltpu.SemaphoreType.DMA((remotes,)),
            pltpu.SemaphoreType.DMA((64,)),
            pltpu.SemaphoreType.DMA((32,)),
            pltpu.SemaphoreType.DMA,
        ],
        compiler_params=pltpu.CompilerParams(
            collective_id=1, has_side_effects=True, vmem_limit_bytes=60 * 1024 * 1024
        ),
        name="forward_and_gather",
    )(*own, *biases, *vecs, lengths, x, patch_rows)
    n = ARRAYS
    got, (text_out, join_out, e, pf), kept = outs[:n], outs[n : n + 4], outs[n + 4 :]
    return got, text_out, join_out, e, pf, kept


(
    GRAD_CONTRACT_TWO,
    GRAD_EXPAND_TWO,
    GRAD_CROSS,
    GRAD_TWO,
    GRAD_CONTRACT_ONE,
    GRAD_EXPAND_ONE,
    GRAD_ONE,
) = range(7)


def backward_kernel(sizes, *refs):
    n_tensor, n_dp, items, slots, patches, padded, width, chunk, counts = sizes
    refs = list(refs)

    def take(n):
        got, refs[:n] = refs[:n], []
        return got

    own, got = take(ARRAYS), take(ARRAYS)
    e_in, pf_in, x, text_out, text_cot, join_cot = take(6)
    vecs_in = take(6)
    self_in = [take(5), take(5)]
    cross_in = take(5)
    feed_in = [take(2), take(2)]
    keeps, sends, outs = take(7), take(7), take(7)
    small_out, grad_text, dpf = take(3)
    wbuf, wk, stage_buf, e_s, ub, dob, acc, pacc, pf, vecs = take(10)
    q_b, k_b, v_b, a_b, p_b = self_buf = take(5)
    qc_b, kc_b, vc_b, ac_b, pc_b = cross_buf = take(5)
    h_b, slope_b = take(2)
    q_s, k_s, v_s, da_s, dq_s, dk_s, dv_s = take(7)
    dkv_s, small_keep, small_send = take(3)
    fetch_sem, store_sem, e_sem, pf_sem = take(4)
    model = x.shape[1]
    hidden = own[EXPAND_ONE].shape[1]
    side = pf.shape[1] - model

    sums = Sums(
        n_tensor,
        n_dp,
        counts,
        chunk,
        sends,
        keeps,
        outs,
        (small_send, small_keep, small_out),
        refs,
    )

    norm_rows(vecs, vecs_in[0:3], vecs_in[3:6])
    pf_copy = pltpu.make_async_copy(pf_in, pf, pf_sem)
    e_copies = [
        pltpu.make_async_copy(e_in.at[n], e_s.at[n], e_sem.at[n]) for n in range(5)
    ]
    for n in (4, 3, 2, 1, 0):
        e_copies[n].start()
    pf_copy.start()

    units = []
    for layer in (1, 0):
        expand, contract = ((EXPAND_ONE, CONTRACT_ONE), (EXPAND_TWO, CONTRACT_TWO))[layer]
        for r in range(4):
            units.append(("contract", layer, r, [(feed_in[layer][0].at[r], h_b)]))
        for r in range(4):
            units.append(
                (
                    "expand",
                    layer,
                    r,
                    [
                        (contract, 0, hidden, wbuf, hidden),
                        (expand, 0, model, wbuf, 0),
                        (feed_in[layer][1].at[r], slope_b),
                    ],
                )
            )
        for r in range(4):
            if layer == 1:
                units.append(
                    (
                        "cross",
                        0,
                        r,
                        [
                            (CROSS_OUT, 0, width, wbuf, width),
                            (JOIN_IN, 3 * width, width, wbuf, 0),
                            (KEY_VALUE, 0, 2 * width, wk, 0),
                        ]
                        + [(cross_in[n].at[r], cross_buf[n]) for n in (3, 0, 1, 2, 4)],
                    )
                )
        for r in range(4):
            first, last = ((TEXT_IN, TEXT_OUT), (JOIN_IN, JOIN_OUT))[layer]
            units.append(
                (
                    "self",
                    layer,
                    r,
                    [(last, 0, width, wbuf, 3 * width), (first, 0, 3 * width, wbuf, 0)]
                    + [(self_in[layer][n].at[r], self_buf[n]) for n in (4, 0, 1, 2, 3)],
                )
            )
    position = {unit[:3]: n for n, unit in enumerate(units)}

    def fetches(n):
        _, _, r, wanted = units[n]
        parity = n % 2
        copies = []
        for i, item in enumerate(wanted):
            if len(item) == 5:
                a, low, count, target, row = item
                source = (own[a] if r == 0 else got[a].at[r - 1]).at[pl.ds(low, count)]
                target = target.at[parity, pl.ds(row, count)]
            else:
                source, target = item
                target = target.at[parity]
            copies.append(pltpu.make_async_copy(source, target, fetch_sem.at[parity, i]))
        return copies

    def begin(n):
        if n + 1 < len(units):
            for copy in fetches(n + 1):
                copy.start()
        for copy in fetches(n):
            copy.wait()
        return n % 2

    stores = {}

    def room(r):
        j = r % 2
        if stores.get(j) is not None:
            stores[j].wait()
            stores[j] = None
        return j

    def put(array, r):
        j = r % 2
        target = (keeps, sends)[j][array]
        rows = target.shape[1]
        stores[j] = pltpu.make_async_copy(
            stage_buf.at[j, pl.ds(0, rows)], target.at[r // 2], store_sem.at[j]
        )
        stores[j].start()

    def settle():
        for j in (0, 1):
            room(j)

    def small_row(r, row, value):
        target = (small_keep, small_send)[r % 2]
        n = 8 * (r // 2) + row
        target[n : n + 1, 0 : value.shape[1]] = value

    def open_layer(n, dy):
        e_copies[n].wait()
        de, partial = norm_backward(e_s[n], vecs[n, 1:2], dy)
        for target in (small_keep, small_send):
            target[16 + 3 * n : 19 + 3 * n] = partial
        dob[...] = de.astype(BF)
        acc[...] = de

    def input_rows(n):
        ub[...] = norm_forward(e_s[n], vecs[n, 1:2], vecs[n, 2:3]).astype(BF)

    def contract_unit(layer, r):
        b = begin(position["contract", layer, r])
        j = room(r)
        stage_buf[j, 0:hidden] = dot_tn(h_b[b], dob[...]).astype(BF)
        put((GRAD_CONTRACT_ONE, GRAD_CONTRACT_TWO)[layer], r)

    def expand_unit(layer, r):
        b = begin(position["expand", layer, r])
        dh = dot_nt(dob[...], wbuf[b, hidden : 2 * hidden])
        dz = (dh * slope_b[b].astype(F32)).astype(BF)
        j = room(r)
        stage_buf[j, 0:model] = dot_tn(ub[...], dz).astype(BF)
        put((GRAD_EXPAND_ONE, GRAD_EXPAND_TWO)[layer], r)
        small_row(r, 6 + layer, jnp.sum(dz.astype(F32), axis=0, keepdims=True))
        acc[...] += dot_nt(dz, wbuf[b, 0:model])

    masks = head_masks(width)

    def self_unit(layer, r):
        b = begin(position["self", layer, r])
        da_s[...] = dot_nt(dob[...], wbuf[b, 3 * width : 4 * width])
        j = room(r)
        stage_buf[j, 3 * width : 4 * width] = dot_tn(a_b[b], dob[...]).astype(BF)
        q_s[...], k_s[...], v_s[...] = (
            q_b[b].astype(F32),
            k_b[b].astype(F32),
            v_b[b].astype(F32),
        )
        for i in range(items):
            rows = pl.ds(i * slots, slots)
            dq, dk, dv = item_backward(
                q_s[rows],
                k_s[rows].astype(BF),
                v_s[rows].astype(BF),
                da_s[rows],
                p_b[b, i],
                masks,
            )
            dq_s[rows], dk_s[rows], dv_s[rows] = dq, dk, dv
        xb = ub[...]
        total = acc[...]
        for c, part in enumerate((dq_s, dk_s, dv_s)):
            pb = part[...].astype(BF)
            stage_buf[j, c * width : (c + 1) * width] = dot_tn(pb, xb).astype(BF)
            total = total + dot_nn(pb, wbuf[b, c * width : (c + 1) * width])
            if c != 1:
                small_row(
                    r, 2 * layer + c // 2, jnp.sum(pb.astype(F32), axis=0, keepdims=True)
                )
        acc[...] = total
        put((GRAD_ONE, GRAD_TWO)[layer], r)

    def cross_unit(r):
        b = begin(position["cross", 0, r])
        da_s[...] = dot_nt(dob[...], wbuf[b, width : 2 * width])
        j = room(r)
        stage_buf[j, width : 2 * width] = dot_tn(ac_b[b], dob[...]).astype(BF)
        q_s[...] = qc_b[b].astype(F32)
        vsum = jnp.zeros((1, width), F32)
        for i in range(items):
            rows = pl.ds(i * slots, slots)
            keys = pl.ds(i * padded, padded)
            dq, dk, dv = item_backward(
                q_s[rows], kc_b[b, keys], vc_b[b, keys], da_s[rows], pc_b[b, i], masks
            )
            dq_s[rows] = dq
            dkv_s[0, keys] = dk.astype(BF)
            dvb = dv.astype(BF)
            dkv_s[1, keys] = dvb
            vsum = vsum + jnp.sum(dvb.astype(F32), axis=0, keepdims=True)
        ticks(1)
        dqb = dq_s[...].astype(BF)
        stage_buf[j, 0:width] = dot_tn(dqb, ub[...]).astype(BF)
        acc[...] += dot_nn(dqb, wbuf[b, 0:width])
        small_row(r, 4, jnp.sum(dqb.astype(F32), axis=0, keepdims=True))
        small_row(r, 5, vsum)
        tails = []
        for c in range(2):
            part = dkv_s[c]
            grad = dot_tn(part, pf[...]).astype(BF)
            stage_buf[j, (2 + c) * width : (3 + c) * width] = grad[:, 0:model]
            tails.append(grad[:, model:])
            back = dot_nn(part, wk[b, c * width : (c + 1) * width])
            for n in range(pacc.shape[0]):
                lanes = back[:, n * 128 : (n + 1) * 128]
                if r == 0 and c == 0:
                    pacc[n] = lanes
                else:
                    pacc[n] += lanes
        tail = jnp.concatenate(tails, axis=0)
        count = tail.shape[0] // (model // side)
        for c in range(model // side):
            stage_buf[j, 4 * width : 4 * width + count, c * side : (c + 1) * side] = tail[
                c * count : (c + 1) * count
            ]
        extra = stage_buf.shape[1] - 4 * width - count
        if extra > 0:
            stage_buf[j, 4 * width + count :] = jnp.zeros((extra, model), BF)
        put(GRAD_CROSS, r)

    small_keep[...] = jnp.zeros_like(small_keep)
    small_send[...] = jnp.zeros_like(small_send)
    for copy in fetches(0):
        copy.start()
    open_layer(4, join_cot[...].astype(F32))
    sums.greet()
    clock = [0]

    def ticks(count):
        for _ in range(count):
            sums.tick(clock[0])
            clock[0] += 1

    def collected(n):
        e_copies[n].wait()
        e_copies[n] = Done()

    for r in range(4):
        contract_unit(1, r)
    settle()
    ticks(1)
    collected(3)
    input_rows(3)
    for r in range(4):
        expand_unit(1, r)
        if r == 3:
            settle()
        ticks(1)
    open_layer(3, acc[...])
    collected(2)
    input_rows(2)
    pf_copy.wait()
    for r in range(4):
        cross_unit(r)
        if r == 3:
            settle()
        ticks(1)
    open_layer(2, acc[...])
    ub[...] = text_out[...]
    for r in range(4):
        self_unit(1, r)
        if r == 3:
            settle()
        ticks((1, 2, 1, 2)[r])
    open_layer(1, acc[...] + text_cot[...].astype(F32))
    for r in range(4):
        contract_unit(0, r)
    settle()
    ticks(1)
    collected(0)
    input_rows(0)
    for r in range(4):
        expand_unit(0, r)
        if r == 3:
            settle()
        ticks(1)
    open_layer(0, acc[...])
    ub[...] = x[...]
    for r in range(4):
        self_unit(0, r)
        if r == 3:
            settle()
        ticks((1, 2, 1, 2)[r])
    grad_text[...] = acc[...].astype(BF)

    def gather_patches(n, carry):
        for c in range(pacc.shape[0]):
            dpf[n, :, c * 128 : (c + 1) * 128] = pacc[
                c, pl.ds(n, items, stride=padded)
            ].astype(BF)
        return carry

    lax.fori_loop(0, patches, gather_patches, 0)
    sums.finish(clock[0])


class Done:
    def wait(self):
        pass


def backward_all(links, own, got, e, pf, x, text_out, cots, vecs, kept, patches, items, width):
    rows, model = x.shape
    slots, padded = rows // items, pf.shape[0] // items
    hidden = own[EXPAND_ONE].shape[1]
    heads = width // HEAD_DIM
    chunk = links.chunk
    anywhere = pl.BlockSpec(memory_space=ANY)
    vmem = pl.BlockSpec(memory_space=pltpu.VMEM)
    cross_rows = 2 * width + 2 * width * pf.shape[1] // model
    extents = [hidden, model, cross_rows, 4 * width, hidden, model, 4 * width]
    extents = [-(-extent // chunk) * chunk for extent in extents]
    counts = tuple(extent // chunk for extent in extents)
    sizes = (links.tensor, links.dp, items, slots, patches, padded, width, chunk, counts)
    pairs = [((2, extent, model), BF) for extent in extents]
    totals = [((extent, model), BF) for extent in extents]
    units, small = 8, 32
    outputs = pairs * 2 + totals
    outputs += [
        ((small - units, model), F32),
        ((rows, model), BF),
        ((patches, items, pf.shape[1]), BF),
    ]
    f32_rows = pltpu.VMEM((rows, width), F32)
    outs = pl.pallas_call(
        functools.partial(backward_kernel, sizes),
        in_specs=[anywhere] * (2 * ARRAYS + 2) + [vmem] * 10 + [anywhere] * len(kept),
        out_specs=[anywhere] * 21 + [vmem] * 3,
        out_shape=[jax.ShapeDtypeStruct(shape, dtype) for shape, dtype in outputs],
        scratch_shapes=[
            pltpu.VMEM((2, 2 * hidden, model), BF),
            pltpu.VMEM((2, 2 * width, pf.shape[1]), BF),
            pltpu.VMEM((2, max(extents), model), BF),
            pltpu.VMEM((5, rows, model), F32),
            pltpu.VMEM((rows, model), BF),
            pltpu.VMEM((rows, model), BF),
            pltpu.VMEM((rows, model), F32),
            pltpu.VMEM((pf.shape[1] // 128, pf.shape[0], 128), F32),
            pltpu.VMEM(pf.shape, BF),
            pltpu.VMEM((5, 3, model), F32),
        ]
        + [pltpu.VMEM((2, rows, width), BF)] * 4
        + [pltpu.VMEM((2, items, heads * slots, slots), BF)]
        + [pltpu.VMEM((2, rows, width), BF)]
        + [pltpu.VMEM((2, pf.shape[0], width), BF)] * 2
        + [pltpu.VMEM((2, rows, width), BF)]
        + [pltpu.VMEM((2, items, heads * slots, padded), BF)]
        + [pltpu.VMEM((2, rows, hidden), BF)] * 2
        + [f32_rows] * 7
        + [
            pltpu.VMEM((2, pf.shape[0], width), BF),
            pltpu.VMEM((small, model), F32),
            pltpu.VMEM((small, model), F32),
            pltpu.SemaphoreType.DMA((2, 8)),
            pltpu.SemaphoreType.DMA((2,)),
            pltpu.SemaphoreType.DMA((5,)),
            pltpu.SemaphoreType.DMA,
        ]
        + Sums.scratch(links.dp, chunk, model, small, units),
        compiler_params=pltpu.CompilerParams(
            collective_id=0, has_side_effects=True, vmem_limit_bytes=60 * 1024 * 1024
        ),
        name="backward_and_sums",
    )(*own, *got, e, pf, x, text_out, *cots, *vecs, *kept)
    return outs[14:21], outs[21], outs[22], outs[23]


def finish_kernel(width, *refs):
    refs = list(refs)

    def take(n):
        got, refs[:n] = refs[:n], []
        return got

    totals, passed, (small,) = take(7), take(4), take(1)
    passed_out = take(4)
    text_in, text_out, expand_one, contract_one, join_in = take(5)
    join_out, cross_out, key_value, expand_two, contract_two = take(5)
    text_bias, join_bias, hidden_one, hidden_two = take(4)
    text_shared, join_shared = take(3), take(3)
    half, full, keys = take(3)
    bounced = take(4)
    load_sem, store_sem = take(2)
    model = full.shape[2]
    side = keys.shape[1] - model
    count = 2 * width * side // model

    loads, stores = [], []
    for n in range(7):
        rows = totals[n].shape[0]
        loads.append(
            pltpu.make_async_copy(totals[n], half.at[n, pl.ds(0, rows)], load_sem.at[n])
        )
        loads[n].start()
    for n in range(4):
        loads.append(pltpu.make_async_copy(passed[n], bounced[n], load_sem.at[7 + n]))
        loads[7 + n].start()

    def store(source, target):
        copy = pltpu.make_async_copy(source, target, store_sem.at[len(stores)])
        copy.start()
        stores.append(copy)

    text_bias[...] = small[0:2, 0:width]
    join_bias[...] = small[2:6, 0:width]
    hidden_one[...] = small[6]
    hidden_two[...] = small[7]
    for n in range(5):
        for c in range(3):
            row = 8 + 3 * n + c
            target, m = (text_shared[c], n) if n < 2 else (join_shared[c], n - 2)
            target[m : m + 1] = small[row : row + 1]

    def widen(n):
        loads[n].wait()
        rows = totals[n].shape[0]
        full[n, 0:rows] = half[n, 0:rows].astype(F32)

    def send(n, lo, rows, target):
        store(full.at[n, pl.ds(lo, rows)], target)

    for n, target in (
        (GRAD_CONTRACT_TWO, contract_two),
        (GRAD_EXPAND_TWO, expand_two),
        (GRAD_CONTRACT_ONE, contract_one),
        (GRAD_EXPAND_ONE, expand_one),
    ):
        widen(n)
        send(n, 0, target.shape[0], target)
    widen(GRAD_CROSS)
    send(GRAD_CROSS, 0, width, join_in.at[pl.ds(3 * width, width)])
    send(GRAD_CROSS, width, width, cross_out)
    keys[:, 0:model] = full[GRAD_CROSS, 2 * width : 4 * width]
    for c in range(model // side):
        keys[c * count : (c + 1) * count, model:] = full[
            GRAD_CROSS, 4 * width : 4 * width + count, c * side : (c + 1) * side
        ]
    store(keys, key_value)
    widen(GRAD_TWO)
    send(GRAD_TWO, 0, 3 * width, join_in.at[pl.ds(0, 3 * width)])
    send(GRAD_TWO, 3 * width, width, join_out)
    widen(GRAD_ONE)
    send(GRAD_ONE, 0, 3 * width, text_in)
    send(GRAD_ONE, 3 * width, width, text_out)
    for n in range(4):
        loads[7 + n].wait()
        store(bounced[n], passed_out[n])
    for copy in stores:
        copy.wait()


def finish_all(totals, passed, small, width, hidden, features):
    model = totals[0].shape[1]
    anywhere = pl.BlockSpec(memory_space=ANY)
    vmem = pl.BlockSpec(memory_space=pltpu.VMEM)
    big = [
        (3 * width, model),
        (width, model),
        (model, hidden),
        (hidden, model),
        (4 * width, model),
        (width, model),
        (width, model),
        (2 * width, features),
        (model, hidden),
        (hidden, model),
    ]
    little = [(2, width), (4, width), (hidden,), (hidden,)]
    little += [(2, model)] * 3 + [(3, model)] * 3
    most = max(total.shape[0] for total in totals)
    return pl.pallas_call(
        functools.partial(finish_kernel, width),
        in_specs=[anywhere] * 11 + [vmem],
        out_specs=[anywhere] * (4 + len(big)) + [vmem] * len(little),
        out_shape=[jax.ShapeDtypeStruct(a.shape, a.dtype) for a in passed]
        + [jax.ShapeDtypeStruct(shape, F32) for shape in big + little],
        scratch_shapes=[
            pltpu.VMEM((7, most, model), BF),
            pltpu.VMEM((7, most, model), F32),
            pltpu.VMEM((2 * width, features), F32),
        ]
        + [pltpu.VMEM(a.shape, a.dtype) for a in passed]
        + [
            pltpu.SemaphoreType.DMA((11,)),
            pltpu.SemaphoreType.DMA((16,)),
        ],
        compiler_params=pltpu.CompilerParams(vmem_limit_bytes=60 * 1024 * 1024),
        name="finish",
    )(*totals, *passed, small)


class Links:
    def __init__(self, mesh):
        self.tensor = mesh.shape["tensor"]
        self.dp = mesh.shape["dp"]
        self.bits = self.dp.bit_length() - 1
        self.chunk = 128


def turned(array):
    array = jnp.swapaxes(array, 1, 2)
    return array.reshape(-1, array.shape[2])


def turned_back(rows, units):
    return jnp.swapaxes(rows.reshape(-1, units, rows.shape[1]), 1, 2)


def per_device(
    links,
    text_rows,
    patch_features,
    lengths,
    text_cotangent,
    join_cotangent,
    text_project_in,
    text_project_bias,
    text_project_out,
    text_expand,
    text_expand_bias,
    text_contract,
    text_out_bias,
    text_norm_gain,
    text_norm_shift,
    join_project_in,
    join_project_bias,
    join_project_out,
    cross_project_out,
    cross_key_value,
    join_expand,
    join_expand_bias,
    join_contract,
    join_out_bias,
    join_norm_gain,
    join_norm_shift,
):
    items, slots, model = text_rows.shape
    patches, patch_width = patch_features.shape[1:]
    width = text_project_in.shape[2]
    hidden = text_expand.shape[1]

    own = [
        turned(text_project_in),
        text_project_out,
        text_expand,
        text_contract,
        turned(join_project_in),
        join_project_out,
        turned(cross_key_value),
        cross_project_out,
        join_expand,
        join_contract,
    ]
    biases = (text_project_bias, join_project_bias, text_expand_bias, join_expand_bias)
    vecs = (text_out_bias, text_norm_gain, text_norm_shift)
    vecs += (join_out_bias, join_norm_gain, join_norm_shift)
    x = text_rows.reshape(items * slots, model)
    text_cot = text_cotangent.reshape(items * slots, model)
    join_cot = join_cotangent.reshape(items * slots, model)
    patch_rows = jnp.swapaxes(patch_features, 0, 1)

    got, text_out, join_out, e, pf, kept = forward_all(
        links, own, biases, vecs, lengths, x, patch_rows, width
    )
    totals, small, grad_text, grad_patches = backward_all(
        links, own, got, e, pf, x, text_out, (text_cot, join_cot), vecs, kept, patches, items, width
    )
    outs = finish_all(
        totals, (text_out, join_out, grad_text, grad_patches), small, width, hidden, patch_width
    )
    text_out, join_out, grad_text, grad_patches = outs[:4]
    text_in, text_project, expand_one, contract_one, join_in = outs[4:9]
    join_project, cross_project, key_value, expand_two, contract_two = outs[9:14]
    text_bias, join_bias, hidden_one, hidden_two = outs[14:18]

    return (
        text_out.reshape(text_rows.shape),
        join_out.reshape(text_rows.shape),
        grad_text.reshape(text_rows.shape),
        jnp.swapaxes(grad_patches, 0, 1),
        turned_back(text_in, width),
        text_bias,
        text_project,
        expand_one,
        hidden_one,
        contract_one,
        *outs[18:21],
        turned_back(join_in, width),
        join_bias,
        join_project,
        cross_project,
        turned_back(key_value, width),
        expand_two,
        hidden_two,
        contract_two,
        *outs[21:24],
    )


def solution(mesh):
    rows = P(("dp", "tensor"), None, None)
    last = P(None, None, "tensor")
    second = P(None, "tensor")
    first = P("tensor", None)
    line = P("tensor")
    full = P()
    in_specs = (
        (rows, rows, P(("dp", "tensor")), rows, rows)
        + (last, second, first, second, line, first, full, full, full)
        + (last, second, first, first, last, second, line, first, full, full, full)
    )
    out_specs = (
        (rows, rows, rows, rows)
        + (last, second, first, second, line, first, full, full, full)
        + (last, second, first, first, last, second, line, first, full, full, full)
    )
    return jax.shard_map(
        functools.partial(per_device, Links(mesh)),
        mesh=mesh,
        in_specs=in_specs,
        out_specs=out_specs,
        check_vma=False,
    )
```

profile of v0, /device:TPU:0, one launch (start us, length us, event | category | flops | bytes accessed | tf_op | source)
XLA Modules:
  0.0 366.4 jit_solution(7580580257709144792)
XLA Ops:
  0.7 113.9 %forward_and_gather.1 = (bf16[3,576,768]{2,1,0:T(8,128)(2,1)}, bf16[3,192,768]{2,1,0:T(8,128)(2,1)}, bf16[3,768,768]{2,1,0:T(8,128)(2,1)}, bf16[3,768,768]{2,1,0...) custom-call(bf16[576,768]{1,0:T(8,128)(2,1)} %bitcast.28, ...), custom_call_target="tpu_custom_call" | custom-call | tf_op jit(solution)/shard_map/forward_and_gather/pallas_call | solution.py:845
  114.6 238.4 %backward_and_sums.1 = (bf16[2,768,768]{2,1,0:T(8,128)(2,1)}, bf16[2,768,768]{2,1,0:T(8,128)(2,1)}, bf16[2,896,768]{2,1,0:T(8,128)(2,1)}, bf16[2,768,768]{2,1,0:...) custom-call(bf16[576,768]{1,0:T(8,128)(2,1)} %bitcast.29, ...), custom_call_target="tpu_custom_call" | custom-call | tf_op jit(solution)/shard_map/backward_and_sums/pallas_call | solution.py:1256
  353.0 13.0 %finish.1 = (bf16[320,768]{1,0:T(8,128)(2,1)}, bf16[320,768]{1,0:T(8,128)(2,1)}, bf16[320,768]{1,0:T(8,128)(2,1)}, bf16[145,8,1024]{2,1,0:T(8,128)(2,1)}, f32[57...) custom-call(bf16[768,768]{1,0:T(8,128)(2,1)} %get-tuple-element.123., ...), custom_call_target="tpu_custom_call" | custom-call | tf_op jit(solution)/shard_map/finish/pallas_call | solution.py:1402
where the time goes:
time: 370 us; the launch traced here: 366 us
  Pallas kernels  365 us (99%)
    pallas_call x1, Pallas kernels, backward_all(): pl.pallas_call(functools.partial(backward_kernel, sizes), in_specs=[anywh...  238 us
    pallas_call x1, Pallas kernels, forward_all(): pl.pallas_call(functools.partial(forward_kernel, sizes), in_specs=[anywhe...  114 us
    pallas_call x1, Pallas kernels, finish_all(): pl.pallas_call(functools.partial(finish_kernel, width), in_specs=[anywher...  13 us

commit v1 on v0

--- a/solution.py
+++ b/solution.py
@@ -74,24 +74,24 @@
 
 
 def item_forward(q, k, v, masks, length):
-    scores = dot_nt(stack_heads(q, masks), k) * HEAD_DIM ** (-0.5)
-    column = lax.broadcasted_iota(jnp.int32, scores.shape, 1)
-    scores = jnp.where(column < length, scores, -1e30)
-    weights = jnp.exp(scores - jnp.max(scores, axis=-1, keepdims=True))
-    probs = (weights / jnp.sum(weights, axis=-1, keepdims=True)).astype(BF)
-    return probs, merge_heads(dot_nn(probs, v), masks)
+    scores = dot_nt(k, stack_heads(q, masks)) * HEAD_DIM ** (-0.5)
+    row = lax.broadcasted_iota(jnp.int32, scores.shape, 0)
+    scores = jnp.where(row < length, scores, -1e30)
+    weights = jnp.exp(scores - jnp.max(scores, axis=0, keepdims=True))
+    probs = (weights / jnp.sum(weights, axis=0, keepdims=True)).astype(BF)
+    return probs, merge_heads(dot_tn(probs, v), masks)
 
 
 def item_backward(q, k, v, da, probs, masks):
     qs = stack_heads(q, masks)
     das = stack_heads(da, masks)
-    dv = dot_tn(probs, das)
-    dp = dot_nt(das, v)
+    dv = dot_nn(probs, das)
+    dp = dot_nt(v, das)
     p = probs.astype(F32)
-    ds = (p * (dp - jnp.sum(p * dp, axis=-1, keepdims=True))).astype(BF)
+    ds = (p * (dp - jnp.sum(p * dp, axis=0, keepdims=True))).astype(BF)
     scaling = HEAD_DIM ** (-0.5)
-    dq = merge_heads(dot_nn(ds, k), masks) * scaling
-    dk = dot_tn(ds, qs) * scaling
+    dq = merge_heads(dot_tn(ds, k), masks) * scaling
+    dk = dot_nn(ds, qs) * scaling
     return dq, dk, dv
 
 
@@ -720,94 +720,101 @@
     u[...] = x[...].astype(F32)
     ub[...] = x[...]
     open_layer(0)
+    move("s1p s1o e1")
     self_unit(0, 0)
-    move("s1p s1v s1o")
+    move("s1p s2p")
     bias_near.need()
     fetch_self(0, 1)
     self_unit(0, 1)
-    move("e1 s1p k1")
+    move("k1 s1p s1v e1 e2")
     bias_far.need()
     bias_last.advance()
     near_start(EXPAND_ONE, CONTRACT_ONE)
     pf_copy.wait()
     spread_patches(pf_raw, pf_wide, pf, items, padded)
     store(pf, pf_out)
+    move("s2p ckv")
     keys_unit(0)
-    move("s1p e1")
+    move("k1 k2")
     fetch_keys(1)
     keys_unit(1)
-    move("k1 s2p e1 s1p")
     bias_last.need()
-    move("s1v s1o ckv")
+    move("s2o s1o e1")
     near_start(JOIN_IN, JOIN_OUT)
     fetch_self(0, 2)
-    fetch_self(0, 3)
     self_unit(0, 2)
+    move("e2")
     fetch_feed(0, 0)
+    fetch_feed(0, 1)
     self_unit(0, 3)
     self_close(0)
+    move("s2v k1")
     close_layer(0)
     open_layer(1)
-    move("k1 s2p e2 k2")
-    fetch_feed(0, 1)
+    move("s2p e2")
     feed_unit(0, 0)
+    move("e1")
     feed_unit(0, 1)
-    move("e1 s2p e2 k2")
+    move("s2p ckv")
+    fetch_keys(2)
+    keys_unit(2)
+    move("cq co k2")
+    fetch_keys(3)
     fetch_feed(0, 2, True)
     fetch_feed(0, 3, True)
-    move("s2p e2 ckv s2v s2o")
-    fetch_keys(2)
-    fetch_keys(3)
-    keys_unit(2)
     keys_unit(3)
     for source, target in zip(cross_st[1:3], cross_out[1:3]):
         store(source, target)
-    move("k1 e2")
+    move("e2 k1")
     near_start(CROSS_OUT, EXPAND_TWO, CONTRACT_TWO)
-    fetch_contract(0, 2)
+    feed_unit(0, 2)
     fetch_contract(0, 3)
-    feed_unit(0, 2)
     fetch_self(1, 0)
+    fetch_self(1, 1)
     feed_unit(0, 3)
+    move("k2")
     feed_close(0)
     close_layer(1, text_out)
     open_layer(2)
     settle("self")
-    move("s2p k2 cq co")
-    fetch_self(1, 1)
+    move("s2p s2o")
     self_unit(1, 0)
+    move("s2v")
     self_unit(1, 1)
-    move("s2v s2o k2")
     fetch_self(1, 2)
+    fetch_cross(0)
+    fetch_cross(1)
+    self_unit(1, 2)
+    move("k2")
     fetch_self(1, 3)
-    self_unit(1, 2)
-    fetch_cross(0)
     self_unit(1, 3)
     self_close(1)
+    move("cq")
     close_layer(2)
     open_layer(3)
-    move("e2")
-    fetch_cross(1)
     cross_unit(0)
     fetch_feed(1, 0)
+    fetch_feed(1, 1)
     cross_unit(1)
-    move("cq co")
+    move("co")
     fetch_cross(2)
+    cross_unit(2)
     fetch_cross(3)
-    cross_unit(2)
-    fetch_feed(1, 1)
     cross_unit(3)
     for n in (0, 3, 4):
         store(cross_st[n], cross_out[n])
     close_layer(3)
     open_layer(4)
     settle("feed")
+    move("e2")
+    feed_unit(1, 0)
+    fetch_feed(1, 2, True)
+    feed_unit(1, 1)
     move("k2")
-    fetch_feed(1, 2, True)
     fetch_feed(1, 3, True)
-    feed_unit(1, 0)
-    feed_unit(1, 1)
+    fetch_contract(1, 2)
     feed_unit(1, 2)
+    fetch_contract(1, 3)
     feed_unit(1, 3)
     feed_close(1)
     close_layer(4, join_out)
@@ -832,8 +839,8 @@
     sizes = (links.tensor, links.dp, items, slots, patches, padded, width)
     mid = ((4, rows, width), BF)
     key = ((4, items * padded, width), BF)
-    probs = ((4, items, heads * slots, slots), BF)
-    cross_probs = ((4, items, heads * slots, padded), BF)
+    probs = ((4, items, slots, heads * slots), BF)
+    cross_probs = ((4, items, padded, heads * slots), BF)
     feed = ((4, rows, hidden), BF)
     pf = ((items * padded, features), BF)
     self_kept = [mid] * 4 + [probs]
@@ -910,7 +917,7 @@
     feed_in = [take(2), take(2)]
     keeps, sends, outs = take(7), take(7), take(7)
     small_out, grad_text, dpf = take(3)
-    wbuf, wk, stage_buf, e_s, ub, dob, acc, pacc, pf, vecs = take(10)
+    wbuf, wk, stage_buf, e_s, ub, ub_t, dob, acc, pacc, pf, vecs = take(11)
     q_b, k_b, v_b, a_b, p_b = self_buf = take(5)
     qc_b, kc_b, vc_b, ac_b, pc_b = cross_buf = take(5)
     h_b, slope_b = take(2)
@@ -1047,7 +1054,9 @@
         acc[...] = de
 
     def input_rows(n):
-        ub[...] = norm_forward(e_s[n], vecs[n, 1:2], vecs[n, 2:3]).astype(BF)
+        rows = norm_forward(e_s[n], vecs[n, 1:2], vecs[n, 2:3])
+        ub[...] = rows.astype(BF)
+        ub_t[...] = rows.T.astype(BF)
 
     def contract_unit(layer, r):
         b = begin(position["contract", layer, r])
@@ -1060,7 +1069,7 @@
         dh = dot_nt(dob[...], wbuf[b, hidden : 2 * hidden])
         dz = (dh * slope_b[b].astype(F32)).astype(BF)
         j = room(r)
-        stage_buf[j, 0:model] = dot_tn(ub[...], dz).astype(BF)
+        stage_buf[j, 0:model] = dot_nn(ub_t[...], dz).astype(BF)
         put((GRAD_EXPAND_ONE, GRAD_EXPAND_TWO)[layer], r)
         small_row(r, 6 + layer, jnp.sum(dz.astype(F32), axis=0, keepdims=True))
         acc[...] += dot_nt(dz, wbuf[b, 0:model])
@@ -1127,17 +1136,16 @@
         small_row(r, 5, vsum)
         tails = []
         for c in range(2):
-            part = dkv_s[c]
-            grad = dot_tn(part, pf[...]).astype(BF)
+            grad = dot_tn(dkv_s[c], pf[...]).astype(BF)
             stage_buf[j, (2 + c) * width : (3 + c) * width] = grad[:, 0:model]
             tails.append(grad[:, model:])
-            back = dot_nn(part, wk[b, c * width : (c + 1) * width])
-            for n in range(pacc.shape[0]):
-                lanes = back[:, n * 128 : (n + 1) * 128]
-                if r == 0 and c == 0:
-                    pacc[n] = lanes
-                else:
-                    pacc[n] += lanes
+        back = dot_nn(dkv_s[0], wk[b, 0:width]) + dot_nn(dkv_s[1], wk[b, width : 2 * width])
+        for n in range(pacc.shape[0]):
+            lanes = back[:, n * 128 : (n + 1) * 128]
+            if r == 0:
+                pacc[n] = lanes
+            else:
+                pacc[n] += lanes
         tail = jnp.concatenate(tails, axis=0)
         count = tail.shape[0] // (model // side)
         for c in range(model // side):
@@ -1172,11 +1180,12 @@
     ticks(1)
     collected(3)
     input_rows(3)
+    ticks(1)
     for r in range(4):
         expand_unit(1, r)
         if r == 3:
             settle()
-        ticks(1)
+        ticks((1, 1, 1, 0)[r])
     open_layer(3, acc[...])
     collected(2)
     input_rows(2)
@@ -1264,6 +1273,7 @@
             pltpu.VMEM((2, max(extents), model), BF),
             pltpu.VMEM((5, rows, model), F32),
             pltpu.VMEM((rows, model), BF),
+            pltpu.VMEM((model, rows), BF),
             pltpu.VMEM((rows, model), BF),
             pltpu.VMEM((rows, model), F32),
             pltpu.VMEM((pf.shape[1] // 128, pf.shape[0], 128), F32),
@@ -1271,11 +1281,11 @@
             pltpu.VMEM((5, 3, model), F32),
         ]
         + [pltpu.VMEM((2, rows, width), BF)] * 4
-        + [pltpu.VMEM((2, items, heads * slots, slots), BF)]
+        + [pltpu.VMEM((2, items, slots, heads * slots), BF)]
         + [pltpu.VMEM((2, rows, width), BF)]
         + [pltpu.VMEM((2, pf.shape[0], width), BF)] * 2
         + [pltpu.VMEM((2, rows, width), BF)]
-        + [pltpu.VMEM((2, items, heads * slots, padded), BF)]
+        + [pltpu.VMEM((2, items, padded, heads * slots), BF)]
         + [pltpu.VMEM((2, rows, hidden), BF)] * 2
         + [f32_rows] * 7
         + [

time: 370 us -> 360 us (0.973)
  Pallas kernels: 365 us -> 356 us
    pallas_call x1, Pallas kernels: 114 us -> 107 us  [forward_all(): pl.pallas_call(functools.partial(forward_kernel, sizes), in_specs=[anywhe...]
where the time goes in v1:
time: 360 us; the launch traced here: 357 us
  Pallas kernels  356 us (99%)
    pallas_call x1, Pallas kernels, backward_all(): pl.pallas_call(functools.partial(backward_kernel, sizes), in_specs=[anywh...  236 us
    pallas_call x1, Pallas kernels, forward_all(): pl.pallas_call(functools.partial(forward_kernel, sizes), in_specs=[anywhe...  107 us
    pallas_call x1, Pallas kernels, finish_all(): pl.pallas_call(functools.partial(finish_kernel, width), in_specs=[anywher...  13 us

profile of v1, /device:TPU:0, one launch (start us, length us, event | category | flops | bytes accessed | tf_op | source)
XLA Modules:
  0.0 356.8 jit_solution(3769203016051765135)
XLA Ops:
  0.7 107.2 %forward_and_gather.1 = (bf16[3,576,768]{2,1,0:T(8,128)(2,1)}, bf16[3,192,768]{2,1,0:T(8,128)(2,1)}, bf16[3,768,768]{2,1,0:T(8,128)(2,1)}, bf16[3,768,768]{2,1,0...) custom-call(bf16[576,768]{1,0:T(8,128)(2,1)} %bitcast.28, ...), custom_call_target="tpu_custom_call" | custom-call | tf_op jit(solution)/shard_map/forward_and_gather/pallas_call | solution.py:852
  107.9 235.7 %backward_and_sums.1 = (bf16[2,768,768]{2,1,0:T(8,128)(2,1)}, bf16[2,768,768]{2,1,0:T(8,128)(2,1)}, bf16[2,896,768]{2,1,0:T(8,128)(2,1)}, bf16[2,768,768]{2,1,0:...) custom-call(bf16[576,768]{1,0:T(8,128)(2,1)} %bitcast.29, ...), custom_call_target="tpu_custom_call" | custom-call | tf_op jit(solution)/shard_map/backward_and_sums/pallas_call | solution.py:1265
  343.7 13.0 %finish.1 = (bf16[320,768]{1,0:T(8,128)(2,1)}, bf16[320,768]{1,0:T(8,128)(2,1)}, bf16[320,768]{1,0:T(8,128)(2,1)}, bf16[145,8,1024]{2,1,0:T(8,128)(2,1)}, f32[57...) custom-call(bf16[768,768]{1,0:T(8,128)(2,1)} %get-tuple-element.123., ...), custom_call_target="tpu_custom_call" | custom-call | tf_op jit(solution)/shard_map/finish/pallas_call | solution.py:1412

commit v2 on v1

--- a/solution.py
+++ b/solution.py
@@ -61,6 +61,10 @@
     ]
 
 
+def groups(count, most):
+    return [range(i, min(i + most, count)) for i in range(0, count, most)]
+
+
 def stack_heads(rows, masks):
     return jnp.concatenate([rows * mask for mask in masks], axis=0).astype(BF)
 
@@ -73,26 +77,34 @@
     return total
 
 
-def item_forward(q, k, v, masks, length):
-    scores = dot_nt(k, stack_heads(q, masks)) * HEAD_DIM ** (-0.5)
-    row = lax.broadcasted_iota(jnp.int32, scores.shape, 0)
-    scores = jnp.where(row < length, scores, -1e30)
-    weights = jnp.exp(scores - jnp.max(scores, axis=0, keepdims=True))
-    probs = (weights / jnp.sum(weights, axis=0, keepdims=True)).astype(BF)
-    return probs, merge_heads(dot_tn(probs, v), masks)
-
-
-def item_backward(q, k, v, da, probs, masks):
-    qs = stack_heads(q, masks)
-    das = stack_heads(da, masks)
-    dv = dot_nn(probs, das)
-    dp = dot_nt(v, das)
-    p = probs.astype(F32)
-    ds = (p * (dp - jnp.sum(p * dp, axis=0, keepdims=True))).astype(BF)
+def items_forward(operands, masks):
+    stacked = [stack_heads(q, masks) for q, _, _, _ in operands]
+    scores = [dot_nt(k, qs) for qs, (_, k, _, _) in zip(stacked, operands)]
+    row = lax.broadcasted_iota(jnp.int32, scores[0].shape, 0)
+    scores = [
+        jnp.where(row < length, s * HEAD_DIM ** (-0.5), -1e30)
+        for s, (_, _, _, length) in zip(scores, operands)
+    ]
+    most = [jnp.max(s, axis=0, keepdims=True) for s in scores]
+    weights = [jnp.exp(s - m) for s, m in zip(scores, most)]
+    totals = [jnp.sum(w, axis=0, keepdims=True) for w in weights]
+    probs = [(w / t).astype(BF) for w, t in zip(weights, totals)]
+    mixed = [dot_tn(p, v) for p, (_, _, v, _) in zip(probs, operands)]
+    return probs, [merge_heads(m, masks) for m in mixed]
+
+
+def items_backward(operands, masks):
+    qs = [stack_heads(q, masks) for q, _, _, _, _ in operands]
+    das = [stack_heads(da, masks) for _, _, _, da, _ in operands]
+    dp = [dot_nt(v, g) for g, (_, _, v, _, _) in zip(das, operands)]
+    dv = [dot_nn(probs, g) for g, (_, _, _, _, probs) in zip(das, operands)]
+    p = [probs.astype(F32) for _, _, _, _, probs in operands]
+    inner = [jnp.sum(a * b, axis=0, keepdims=True) for a, b in zip(p, dp)]
+    ds = [(a * (b - c)).astype(BF) for a, b, c in zip(p, dp, inner)]
     scaling = HEAD_DIM ** (-0.5)
-    dq = merge_heads(dot_tn(ds, k), masks) * scaling
-    dk = dot_nn(ds, qs) * scaling
-    return dq, dk, dv
+    dk = [dot_nn(s, g) * scaling for s, g in zip(ds, qs)]
+    dq = [dot_tn(s, k) for s, (_, k, _, _, _) in zip(ds, operands)]
+    return [merge_heads(part, masks) * scaling for part in dq], dk, dv
 
 
 def pair(index, width):
@@ -620,13 +632,18 @@
         ).astype(BF)
         q_st[r], k_st[r], v_st[r] = q, k, v
         q_s[...], k_s[...], v_s[...] = q.astype(F32), k.astype(F32), v.astype(F32)
-        for i in range(items):
-            rows = pl.ds(i * slots, slots)
-            probs, a = item_forward(
-                q_s[rows], k_s[rows].astype(BF), v_s[rows].astype(BF), masks, lengths[i]
+        for group in groups(items, 8):
+            spans = [pl.ds(i * slots, slots) for i in group]
+            probs, mixed = items_forward(
+                [
+                    (q_s[rows], k_s[rows].astype(BF), v_s[rows].astype(BF), lengths[i])
+                    for i, rows in zip(group, spans)
+                ],
+                masks,
             )
-            p_st[r, i] = probs
-            a_s[rows] = a
+            for n, i in enumerate(group):
+                p_st[r, i] = probs[n]
+                a_s[spans[n]] = mixed[n]
         ab = a_s[...].astype(BF)
         a_st[r] = ab
         acc[...] += dot_nn(ab, ws[r, 3 * width : 4 * width])
@@ -690,12 +707,19 @@
         q = (dot_nt(ub[...], wc[r, 0:width]) + bias[r, 4:5, 0:width]).astype(BF)
         qc_st[r] = q
         q_s[...] = q.astype(F32)
-        for i in range(items):
-            rows = pl.ds(i * slots, slots)
-            keys = pl.ds(i * padded, padded)
-            probs, a = item_forward(q_s[rows], kc_st[r, keys], vc_st[r, keys], masks, patches)
-            pc_st[r, i] = probs
-            a_s[rows] = a
+        for group in groups(items, 4):
+            spans = [pl.ds(i * slots, slots) for i in group]
+            keys = [pl.ds(i * padded, padded) for i in group]
+            probs, mixed = items_forward(
+                [
+                    (q_s[rows], kc_st[r, part], vc_st[r, part], patches)
+                    for rows, part in zip(spans, keys)
+                ],
+                masks,
+            )
+            for n, i in enumerate(group):
+                pc_st[r, i] = probs[n]
+                a_s[spans[n]] = mixed[n]
         ab = a_s[...].astype(BF)
         ac_st[r] = ab
         acc[...] += dot_nn(ab, wc[r, width:middle])
@@ -1086,17 +1110,23 @@
             k_b[b].astype(F32),
             v_b[b].astype(F32),
         )
-        for i in range(items):
-            rows = pl.ds(i * slots, slots)
-            dq, dk, dv = item_backward(
-                q_s[rows],
-                k_s[rows].astype(BF),
-                v_s[rows].astype(BF),
-                da_s[rows],
-                p_b[b, i],
+        for group in groups(items, 8):
+            spans = [pl.ds(i * slots, slots) for i in group]
+            dq, dk, dv = items_backward(
+                [
+                    (
+                        q_s[rows],
+                        k_s[rows].astype(BF),
+                        v_s[rows].astype(BF),
+                        da_s[rows],
+                        p_b[b, i],
+                    )
+                    for i, rows in zip(group, spans)
+                ],
                 masks,
             )
-            dq_s[rows], dk_s[rows], dv_s[rows] = dq, dk, dv
+            for n, rows in enumerate(spans):
+                dq_s[rows], dk_s[rows], dv_s[rows] = dq[n], dk[n], dv[n]
         xb = ub[...]
         total = acc[...]
         for c, part in enumerate((dq_s, dk_s, dv_s)):
@@ -1117,17 +1147,22 @@
         stage_buf[j, width : 2 * width] = dot_tn(ac_b[b], dob[...]).astype(BF)
         q_s[...] = qc_b[b].astype(F32)
         vsum = jnp.zeros((1, width), F32)
-        for i in range(items):
-            rows = pl.ds(i * slots, slots)
-            keys = pl.ds(i * padded, padded)
-            dq, dk, dv = item_backward(
-                q_s[rows], kc_b[b, keys], vc_b[b, keys], da_s[rows], pc_b[b, i], masks
+        for group in groups(items, 4):
+            spans = [pl.ds(i * slots, slots) for i in group]
+            keys = [pl.ds(i * padded, padded) for i in group]
+            dq, dk, dv = items_backward(
+                [
+                    (q_s[rows], kc_b[b, part], vc_b[b, part], da_s[rows], pc_b[b, i])
+                    for i, rows, part in zip(group, spans, keys)
+                ],
+                masks,
             )
-            dq_s[rows] = dq
-            dkv_s[0, keys] = dk.astype(BF)
-            dvb = dv.astype(BF)
-            dkv_s[1, keys] = dvb
-            vsum = vsum + jnp.sum(dvb.astype(F32), axis=0, keepdims=True)
+            for n, part in enumerate(keys):
+                dq_s[spans[n]] = dq[n]
+                dkv_s[0, part] = dk[n].astype(BF)
+                dvb = dv[n].astype(BF)
+                dkv_s[1, part] = dvb
+                vsum = vsum + jnp.sum(dvb.astype(F32), axis=0, keepdims=True)
         ticks(1)
         dqb = dq_s[...].astype(BF)
         stage_buf[j, 0:width] = dot_tn(dqb, ub[...]).astype(BF)

time: 360 us -> 346 us (0.961)
  Pallas kernels: 356 us -> 342 us
    pallas_call x1, Pallas kernels: 236 us -> 228 us  [backward_all(): pl.pallas_call(functools.partial(backward_kernel, sizes), in_specs=[anywh...]
    pallas_call x1, Pallas kernels: 107 us -> 101 us  [forward_all(): pl.pallas_call(functools.partial(forward_kernel, sizes), in_specs=[anywhe...]
where the time goes in v2:
time: 346 us; the launch traced here: 343 us
  Pallas kernels  342 us (99%)
    pallas_call x1, Pallas kernels, backward_all(): pl.pallas_call(functools.partial(backward_kernel, sizes), in_specs=[anywh...  228 us
    pallas_call x1, Pallas kernels, forward_all(): pl.pallas_call(functools.partial(forward_kernel, sizes), in_specs=[anywhe...  101 us
    pallas_call x1, Pallas kernels, finish_all(): pl.pallas_call(functools.partial(finish_kernel, width), in_specs=[anywher...  13 us

profile of v2, /device:TPU:0, one launch (start us, length us, event | category | flops | bytes accessed | tf_op | source)
XLA Modules:
  0.0 343.2 jit_solution(15838049615519784426)
XLA Ops:
  0.7 101.1 %forward_and_gather.1 = (bf16[3,576,768]{2,1,0:T(8,128)(2,1)}, bf16[3,192,768]{2,1,0:T(8,128)(2,1)}, bf16[3,768,768]{2,1,0:T(8,128)(2,1)}, bf16[3,768,768]{2,1,0...) custom-call(bf16[576,768]{1,0:T(8,128)(2,1)} %bitcast.28, ...), custom_call_target="tpu_custom_call" | custom-call | tf_op jit(solution)/shard_map/forward_and_gather/pallas_call | solution.py:876
  101.8 228.3 %backward_and_sums.1 = (bf16[2,768,768]{2,1,0:T(8,128)(2,1)}, bf16[2,768,768]{2,1,0:T(8,128)(2,1)}, bf16[2,896,768]{2,1,0:T(8,128)(2,1)}, bf16[2,768,768]{2,1,0:...) custom-call(bf16[576,768]{1,0:T(8,128)(2,1)} %bitcast.29, ...), custom_call_target="tpu_custom_call" | custom-call | tf_op jit(solution)/shard_map/backward_and_sums/pallas_call | solution.py:1300
  330.0 13.0 %finish.1 = (bf16[320,768]{1,0:T(8,128)(2,1)}, bf16[320,768]{1,0:T(8,128)(2,1)}, bf16[320,768]{1,0:T(8,128)(2,1)}, bf16[145,8,1024]{2,1,0:T(8,128)(2,1)}, f32[57...) custom-call(bf16[768,768]{1,0:T(8,128)(2,1)} %get-tuple-element.123., ...), custom_call_target="tpu_custom_call" | custom-call | tf_op jit(solution)/shard_map/finish/pallas_call | solution.py:1447

commit v3 on v2

--- a/solution.py
+++ b/solution.py
@@ -947,7 +947,7 @@
     h_b, slope_b = take(2)
     q_s, k_s, v_s, da_s, dq_s, dk_s, dv_s = take(7)
     dkv_s, small_keep, small_send = take(3)
-    fetch_sem, store_sem, e_sem, pf_sem = take(4)
+    fetch_sem, store_sem, e_sem, pf_sem, h_sem = take(5)
     model = x.shape[1]
     hidden = own[EXPAND_ONE].shape[1]
     side = pf.shape[1] - model
@@ -971,13 +971,20 @@
     ]
     for n in (4, 3, 2, 1, 0):
         e_copies[n].start()
+    h_copies = [
+        [
+            pltpu.make_async_copy(feed_in[layer][0].at[r], h_b.at[r], h_sem.at[r])
+            for r in range(4)
+        ]
+        for layer in range(2)
+    ]
+    for copy in h_copies[1]:
+        copy.start()
     pf_copy.start()
 
     units = []
     for layer in (1, 0):
         expand, contract = ((EXPAND_ONE, CONTRACT_ONE), (EXPAND_TWO, CONTRACT_TWO))[layer]
-        for r in range(4):
-            units.append(("contract", layer, r, [(feed_in[layer][0].at[r], h_b)]))
         for r in range(4):
             units.append(
                 (
@@ -1051,12 +1058,14 @@
             stores[j] = None
         return j
 
-    def put(array, r):
+    def put(array, r, lo=0, hi=None):
         j = r % 2
         target = (keeps, sends)[j][array]
-        rows = target.shape[1]
+        rows = (target.shape[1] if hi is None else hi) - lo
         stores[j] = pltpu.make_async_copy(
-            stage_buf.at[j, pl.ds(0, rows)], target.at[r // 2], store_sem.at[j]
+            stage_buf.at[j, pl.ds(0, rows)],
+            target.at[r // 2, pl.ds(lo, rows)],
+            store_sem.at[j],
         )
         stores[j].start()
 
@@ -1082,11 +1091,12 @@
         ub[...] = rows.astype(BF)
         ub_t[...] = rows.T.astype(BF)
 
-    def contract_unit(layer, r):
-        b = begin(position["contract", layer, r])
+    def contract_unit(layer, r, lo, hi):
+        if lo == 0:
+            h_copies[layer][r].wait()
         j = room(r)
-        stage_buf[j, 0:hidden] = dot_tn(h_b[b], dob[...]).astype(BF)
-        put((GRAD_CONTRACT_ONE, GRAD_CONTRACT_TWO)[layer], r)
+        stage_buf[j, 0 : hi - lo] = dot_tn(h_b[r, :, lo:hi], dob[...]).astype(BF)
+        put((GRAD_CONTRACT_ONE, GRAD_CONTRACT_TWO)[layer], r, lo, hi)
 
     def expand_unit(layer, r):
         b = begin(position["expand", layer, r])
@@ -1209,18 +1219,23 @@
         e_copies[n].wait()
         e_copies[n] = Done()
 
+    first = 2 * chunk
     for r in range(4):
-        contract_unit(1, r)
+        contract_unit(1, r, 0, first)
     settle()
     ticks(1)
     collected(3)
     input_rows(3)
     ticks(1)
     for r in range(4):
+        contract_unit(1, r, first, hidden)
+    settle()
+    ticks(1)
+    for r in range(4):
         expand_unit(1, r)
         if r == 3:
             settle()
-        ticks((1, 1, 1, 0)[r])
+        ticks((1, 0, 1, 0)[r])
     open_layer(3, acc[...])
     collected(2)
     input_rows(2)
@@ -1232,6 +1247,8 @@
         ticks(1)
     open_layer(2, acc[...])
     ub[...] = text_out[...]
+    for copy in h_copies[0]:
+        copy.start()
     for r in range(4):
         self_unit(1, r)
         if r == 3:
@@ -1239,7 +1256,7 @@
         ticks((1, 2, 1, 2)[r])
     open_layer(1, acc[...] + text_cot[...].astype(F32))
     for r in range(4):
-        contract_unit(0, r)
+        contract_unit(0, r, 0, hidden)
     settle()
     ticks(1)
     collected(0)
@@ -1321,7 +1338,7 @@
         + [pltpu.VMEM((2, pf.shape[0], width), BF)] * 2
         + [pltpu.VMEM((2, rows, width), BF)]
         + [pltpu.VMEM((2, items, padded, heads * slots), BF)]
-        + [pltpu.VMEM((2, rows, hidden), BF)] * 2
+        + [pltpu.VMEM((4, rows, hidden), BF), pltpu.VMEM((2, rows, hidden), BF)]
         + [f32_rows] * 7
         + [
             pltpu.VMEM((2, pf.shape[0], width), BF),
@@ -1331,6 +1348,7 @@
             pltpu.SemaphoreType.DMA((2,)),
             pltpu.SemaphoreType.DMA((5,)),
             pltpu.SemaphoreType.DMA,
+            pltpu.SemaphoreType.DMA((4,)),
         ]
         + Sums.scratch(links.dp, chunk, model, small, units),
         compiler_params=pltpu.CompilerParams(

time: 346 us -> 345 us (level)
  no operation moved by 1% of the time
where the time goes in v3:
time: 345 us; the launch traced here: 341 us
  Pallas kernels  340 us (99%)
    pallas_call x1, Pallas kernels, backward_all(): pl.pallas_call(functools.partial(backward_kernel, sizes), in_specs=[anywh...  226 us
    pallas_call x1, Pallas kernels, forward_all(): pl.pallas_call(functools.partial(forward_kernel, sizes), in_specs=[anywhe...  101 us
    pallas_call x1, Pallas kernels, finish_all(): pl.pallas_call(functools.partial(finish_kernel, width), in_specs=[anywher...  13 us

profile of v3, /device:TPU:0, one launch (start us, length us, event | category | flops | bytes accessed | tf_op | source)
XLA Modules:
  0.0 341.3 jit_solution(3031632840218840868)
XLA Ops:
  0.7 101.1 %forward_and_gather.1 = (bf16[3,576,768]{2,1,0:T(8,128)(2,1)}, bf16[3,192,768]{2,1,0:T(8,128)(2,1)}, bf16[3,768,768]{2,1,0:T(8,128)(2,1)}, bf16[3,768,768]{2,1,0...) custom-call(bf16[576,768]{1,0:T(8,128)(2,1)} %bitcast.28, ...), custom_call_target="tpu_custom_call" | custom-call | tf_op jit(solution)/shard_map/forward_and_gather/pallas_call | solution.py:876
  101.8 226.3 %backward_and_sums.1 = (bf16[2,768,768]{2,1,0:T(8,128)(2,1)}, bf16[2,768,768]{2,1,0:T(8,128)(2,1)}, bf16[2,896,768]{2,1,0:T(8,128)(2,1)}, bf16[2,768,768]{2,1,0:...) custom-call(bf16[576,768]{1,0:T(8,128)(2,1)} %bitcast.29, ...), custom_call_target="tpu_custom_call" | custom-call | tf_op jit(solution)/shard_map/backward_and_sums/pallas_call | solution.py:1317
  328.1 13.0 %finish.1 = (bf16[320,768]{1,0:T(8,128)(2,1)}, bf16[320,768]{1,0:T(8,128)(2,1)}, bf16[320,768]{1,0:T(8,128)(2,1)}, bf16[145,8,1024]{2,1,0:T(8,128)(2,1)}, f32[57...) custom-call(bf16[768,768]{1,0:T(8,128)(2,1)} %get-tuple-element.123., ...), custom_call_target="tpu_custom_call" | custom-call | tf_op jit(solution)/shard_map/finish/pallas_call | solution.py:1465
